TPU v7x, 32 devices: a whole 2x2x4 slice. The times are simulated.
32 devices in a mesh: outer: 2 (over x), sec: 8 (over z, core), tp: 2 (over y).
Axes of the slice: x: 2, y: 2, z: 4, core: 2. Of those that a mesh axis runs over, the one named last changes fastest.
Arguments:
- tile_maps: bfloat16 [32, 12, 12, 3072], P(('outer', 'sec'), None, None, 'tp'), may hold values from -6 to 6
- tile_shape: int32 [32, 2], P(('outer', 'sec')), may hold values from 4 to 12
- conv_kernel: float32 [7, 7, 3072], P(None, None, 'tp'), may hold values from -0.875 to 0.875
- norm_gain: float32 [3072], P('tp'), may hold values from 0.25 to 1.75
- norm_bias: float32 [3072], P('tp'), may hold values from -3 to 3
- projector: bfloat16 [3072, 7168], P('tp', 'sec'), may hold values from -0.109375 to 0.109375
- text_rows: bfloat16 [9216, 7168], P(('outer', 'sec'), 'tp'), may hold values from -6 to 6
- row_order: int32 [16, 576], P(('outer', 'sec')), may hold values from 0 to 575, each once within a row
- seq_gain: float32 [7168], P('tp'), may hold values from 0.25 to 1.75
- cotangent: bfloat16 [9216, 7168], P(('outer', 'sec'), 'tp'), may hold values from -0.2772166 to 0.2772166, as said below
Outputs:
- normed: bfloat16 [9216, 7168], P(('outer', 'sec'), 'tp')
- kernel_delta: float32 [7, 7, 3072], P(None, None, 'tp')
- gain_delta: float32 [3072], P('tp')
- bias_delta: float32 [3072], P('tp')
Inputs may be any that keep to these rules, and one draw needn't show every extreme that they name: `row_order`: each row lists where the visual tokens arriving at that device stand, in arrival order, then the text rows. `tile_shape`: valid rows and columns of each tile, the rest of the map is padding. `cotangent`: gradient of the training loss.
All inputs are finite; a program needn't handle non-finite values.
Results may differ from a plain program's by a relative error of at most 0.0043.
Values may be sent and summed in bfloat16 or wider, within the bound.
A program may use at most 128 MiB of HBM per device.

v0:
```python
import jax
import jax.numpy as jnp
from jax import lax
from jax.sharding import PartitionSpec as P


def shape_mask(tile_shape, grid):
    places = lax.broadcasted_iota(jnp.int32, (1, grid), 1)
    rows_ok = places < tile_shape[:, 0:1]
    cols_ok = places < tile_shape[:, 1:2]
    return (rows_ok[:, :, None] & cols_ok[:, None, :]).astype(jnp.float32)


def on_device(
    tile_maps,
    tile_shape,
    conv_kernel,
    norm_gain,
    norm_bias,
    projector,
    text_rows,
    row_order,
    seq_gain,
    cotangent,
):
    grid = tile_maps.shape[1]
    half_ch = tile_maps.shape[3]
    channels = half_ch * lax.axis_size("tp")
    rows_dev = tile_maps.shape[0] * grid * grid
    width = text_rows.shape[1] * lax.axis_size("tp")
    validity = shape_mask(tile_shape, grid)[..., None]
    masked = tile_maps.astype(jnp.float32) * validity
    padded = jnp.pad(masked, ((0, 0), (3, 3), (3, 3), (0, 0)))
    conv_out = jnp.zeros(masked.shape, jnp.float32)
    for row_off in range(7):
        for col_off in range(7):
            conv_out = (
                conv_out
                + padded[:, row_off : row_off + grid, col_off : col_off + grid, :]
                * conv_kernel[row_off, col_off]
            )
    total_one, total_two = lax.psum(
        (jnp.sum(conv_out, axis=-1), jnp.sum(conv_out * conv_out, axis=-1)), "tp"
    )
    center = (total_one / channels)[..., None]
    inverse = lax.rsqrt((total_two / channels)[..., None] - center * center + 1e-06)
    normal = (conv_out - center) * inverse
    features = (
        (validity * (normal * norm_gain + norm_bias))
        .astype(jnp.bfloat16)
        .reshape(rows_dev, half_ch)
    )
    whole_weight = lax.all_gather(projector, "sec", axis=1, tiled=True)
    partial_value = jnp.dot(features, whole_weight, preferred_element_type=jnp.float32)
    visual = lax.psum_scatter(partial_value, "tp", scatter_dimension=1, tiled=True).astype(
        jnp.bfloat16
    )
    arrived = lax.all_to_all(visual, "sec", split_axis=0, concat_axis=0, tiled=True)
    positions = row_order[0, :rows_dev]
    merged = text_rows.at[positions].set(arrived)
    wide = merged.astype(jnp.float32)
    upstream = cotangent.astype(jnp.float32) * seq_gain
    square_sum, along = lax.psum(
        (jnp.sum(wide * wide, axis=-1), jnp.sum(upstream * wide, axis=-1)), "tp"
    )
    inv_rms = lax.rsqrt(square_sum / width + 1e-05)[:, None]
    normed = (wide * inv_rms * seq_gain).astype(jnp.bfloat16)
    grad_seq = inv_rms * upstream - wide * (inv_rms * inv_rms * inv_rms) * along[:, None] / width
    picked = grad_seq[positions].astype(jnp.bfloat16)
    returned = lax.all_to_all(picked, "sec", split_axis=0, concat_axis=0, tiled=True)
    full_grad = lax.all_gather(returned, "tp", axis=1, tiled=True)
    grad_rows = jnp.dot(full_grad, whole_weight.T, preferred_element_type=jnp.float32)
    masked_grad = grad_rows.reshape(masked.shape) * validity
    scaled = masked_grad * norm_gain
    first_sum, second_sum = lax.psum(
        (jnp.sum(scaled, axis=-1), jnp.sum(scaled * normal, axis=-1)), "tp"
    )
    grad_conv = inverse * (
        scaled - (first_sum / channels)[..., None] - normal * (second_sum / channels)[..., None]
    )
    kernel_rows = []
    for row_off in range(7):
        for col_off in range(7):
            window = padded[:, row_off : row_off + grid, col_off : col_off + grid, :]
            kernel_rows.append(jnp.sum(window * grad_conv, axis=(0, 1, 2)))
    gain_grad = jnp.sum(masked_grad * normal, axis=(0, 1, 2))
    bias_grad = jnp.sum(masked_grad, axis=(0, 1, 2))
    local_delta = jnp.stack(kernel_rows + [gain_grad, bias_grad], axis=0)
    pods = lax.axis_size("outer")
    entries = 51 * channels
    pod_sum = lax.psum(local_delta, "sec")
    norm_sq = lax.psum(jnp.sum(pod_sum * pod_sum), "tp")
    factor = jnp.minimum(1.0, 1.0 / jnp.sqrt(norm_sq / entries + 1e-06))
    average = lax.psum(pod_sum * factor, "outer") / pods
    return (normed, average[:49].reshape(7, 7, half_ch), average[49], average[50])


def solution(mesh):
    in_specs = (
        P(("outer", "sec"), None, None, "tp"),
        P(("outer", "sec"), None),
        P(None, None, "tp"),
        P("tp"),
        P("tp"),
        P("tp", "sec"),
        P(("outer", "sec"), "tp"),
        P(("outer", "sec"), None),
        P("tp"),
        P(("outer", "sec"), "tp"),
    )
    out_specs = (P(("outer", "sec"), "tp"), P(None, None, "tp"), P("tp"), P("tp"))
    return jax.shard_map(
        on_device, mesh=mesh, in_specs=in_specs, out_specs=out_specs, check_vma=False
    )
```

profile of v0, /device:TPU:0, one launch (start us, length us, event | category | flops | bytes accessed | tf_op | source)
XLA Modules:
  0.0 696.8 jit_solution(15552070662868830435)
XLA Ops:
  7.2 4.4 copy.23
  11.7 0.6 copy-done.9
  12.3 0.2 slice_reduce_fusion.52
  12.5 0.1 copy-done.2
  12.6 0.2 slice_reduce_fusion.48
  12.8 0.3 slice_reduce_fusion.50
  13.1 0.9 slice_reduce_fusion.49
  14.2 0.2 convert_multiply_fusion.5
  14.4 23.6 %fusion.8 = (f32[2,12,12]{2,1,0:T(8,128)S(1)}, f32[2,12,12]{2,1,0:T(8,128)S(1)}, f32[2,12,12,1536]{3,2,1,0:T(8,128)}) fusion(f32[1536]{0:T(1024)S(1)} %get-tuple-element.110, f32[1536]{0:T(1024)S(1)} %get-tuple-element.111, f32[1536]{0:T(1024)S(1)} %get-tuple-element.64, f32[1536]{0:T(1024)S(1)} %get-tuple-element.65, f32[1536]{0:T(1024)S(1)} %get-tuple-element.66, ...), kind=kLoop, calls=%fused_computation.189 | loop fusion | flops 44236224 | bytes 3842304 | tf_op jit(solution)/shard_map/reduce_sum | solution.py:43
  38.1 9.8 %all-reduce.3 = (f32[2,12,12]{2,1,0:T(8,128)S(1)}, f32[2,12,12]{2,1,0:T(8,128)S(1)}) all-reduce(f32[2,12,12]{2,1,0:T(8,128)S(1)} %get-tuple-element.58, f32[2,12,12]{2,1,0:T(8,128)S(1)} %get-tuple-element.57), channel_id=1, replica_groups=mesh['outer'=2,'sec'=8,'tp'=2] {'tp'}, use_global_device_ids=true, to_apply=%region_3.4 | all-reduce | flops 576 | bytes 4608 | tf_op jit(solution)/shard_map/psum | solution.py:42
  47.9 0.6 copy-done.3
  48.5 3.5 multiply_convert_fusion
  52.0 1.1 reshape.168
  53.1 155.4 %all-gather.3.cloned.1.call-done = bf16[1536,7168]{1,0:T(8,128)(2,1)} async-done(((bf16[1536,896]{1,0:T(8,128)(2,1)}), bf16[1536,7168]{1,0:T(8,128)(2,1)}) %all-gather.3.cloned.1.call-update) | async-done | bytes 22020112 | tf_op jit(solution)/shard_map/all_gather | solution.py:53
  208.5 13.1 %fusion.9 = f32[288,7168]{1,0:T(8,128)} fusion(bf16[288,1536]{1,0:T(8,128)(2,1)} %reshape.168, bf16[1536,7168]{1,0:T(8,128)(2,1)} %all-gather.3.cloned.1.call-done), kind=kOutput, calls=%fused_computation.190 | convolution fusion | flops 6341787648 | bytes 31162368 | tf_op jit(solution)/shard_map/dot_general | solution.py:54
  221.7 96.2 %reduce-scatter.2.cloned.1.call-done = f32[288,3584]{1,0:T(8,128)} async-done(((f32[288,7168]{1,0:T(8,128)}), f32[288,3584]{1,0:T(8,128)}) %reduce-scatter.2.cloned.1.call-update) | async-done | bytes 4128784 | tf_op jit(solution)/shard_map/reduce_scatter | solution.py:55
  317.8 3.7 convert_element_type.43
  321.6 4.0 all_to_all.14
  325.5 4.7 all-to-all-start
  330.3 0.2 all-gather.5.cloned.1.call-start
  330.5 53.1 %all-to-all-done = bf16[8,36,3584]{2,1,0:T(8,128)(2,1)} async-done(((bf16[8,36,3584]{2,1,0:T(8,128)(2,1)}), bf16[8,36,3584]{2,1,0:T(8,128)(2,1)}, u32[]{:S(2)}, u32[]{:S(2)}) %all-to-all-start) | async-done | bytes 2064416 | tf_op jit(solution)/shard_map/all_to_all | solution.py:58
  383.7 4.0 reshape.184
  387.7 9.2 %scatter_fusion = bf16[576,3584]{1,0:T(8,128)(2,1)} fusion(bf16[576,3584]{1,0:T(8,128)(2,1)} %copy.23, s32[288]{0:T(512)S(1)} %fusion.7, bf16[288,3584]{1,0:T(8,128)(2,1)} %reshape.184), kind=kCustom, calls=%fused_computation.1 | custom fusion | bytes 6194304 | tf_op jit(solution)/shard_map/scatter | solution.py:60
  396.9 5.4 fusion.6
  402.3 5.0 all-reduce.2
  407.3 6.7 fusion.5
  414.0 10.0 %gather_fusion = bf16[288,3584]{1,0:T(8,128)(2,1)} fusion(bf16[576,3584]{1,0:T(8,128)(2,1)} %fusion.5, s32[1024]{0:T(1024)S(1)} %pad_clamp_fusion), kind=kCustom, calls=%fused_computation | custom fusion | bytes 4129920 | tf_op jit(solution)/shard_map/gather | solution.py:69
  424.1 4.0 convert_element_type.48
  428.0 57.6 %all_to_all.21 = bf16[8,36,3584]{2,1,0:T(8,128)(2,1)} all-to-all(bf16[8,36,3584]{2,1,0:T(8,128)(2,1)} %convert_element_type.48), channel_id=1, replica_groups=mesh['outer'=2,'sec'=8,'tp'=2] {'sec'}, dimensions={0} | all-to-all | bytes 4128768 | tf_op jit(solution)/shard_map/all_to_all | solution.py:70
  485.7 4.0 all_to_all.18
  489.8 54.0 %all-gather.5.cloned.1.call-done = bf16[288,7168]{1,0:T(8,128)(2,1)} async-done(((bf16[288,3584]{1,0:T(8,128)(2,1)}), bf16[288,7168]{1,0:T(8,128)(2,1)}) %all-gather.5.cloned.1.call-update) | async-done | bytes 4128784 | tf_op jit(solution)/shard_map/all_gather | solution.py:71
  543.7 13.2 %multiply_reduce_fusion.53 = (f32[1536]{0:T(1024)S(1)}, f32[288]{0:T(512)S(1)}, f32[288,1536]{1,0:T(8,128)}) fusion(f32[288]{0:T(512)S(1)} %reshape.171, f32[1536]{0:T(1024)S(1)} %copy-done.8, bf16[288,7168]{1,0:T(8,128)(2,1)} %all-gather.5.cloned.1.call-done, bf16[1536,7168]{1,0:T(8,128)(2,1)} %all-gather.3.cloned.1.call-done), kind=kOutput, calls=%fused_computation.120 | convolution fusion | flops 6343555072 | bytes 27932928 | tf_op jit(solution)/shard_map/dot_general | solution.py:72
  557.0 2.8 reshape.169
  559.8 3.4 multiply_reduce_fusion
  563.2 7.4 %all-reduce.1 = (f32[2,12,12]{2,1,0:T(8,128)S(1)}, f32[2,12,12]{2,1,0:T(8,128)S(1)}) all-reduce(f32[2,12,12]{2,1,0:T(8,128)S(1)} %get-tuple-element.5, f32[2,12,12]{2,1,0:T(8,128)S(1)} %reduce_sum.529), channel_id=1, replica_groups=mesh['outer'=2,'sec'=8,'tp'=2] {'tp'}, use_global_device_ids=true, to_apply=%region_13.14 | all-reduce | flops 576 | bytes 4608 | tf_op jit(solution)/shard_map/psum | solution.py:75
  570.7 9.6 %multiply_reduce_fusion.1 = (f32[1536]{0:T(1024)S(1)}, f32[1536]{0:T(1024)S(1)}, f32[1536]{0:T(1024)S(1)}, f32[1536]{0:T(1024)S(1)}, f32[1536]{0:T(1024)S(1)}, /...) fusion(f32[2,12,12,1536]{3,2,1,0:T(8,128)S(1)} %convert_multipl, ...), kind=kLoop, calls=%fused_computation.63 | loop fusion | flops 19436544 | bytes 7200384 | tf_op jit(solution)/shard_map/reduce_sum | solution.py:85
  580.3 6.3 multiply_reduce_fusion.19
  586.6 5.4 multiply_reduce_fusion.38
  592.8 4.8 stack.207
  597.7 54.4 %all-reduce.7.cloned.1.call-done = f32[51,1536]{1,0:T(8,128)} async-done(((f32[51,1536]{1,0:T(8,128)}), f32[51,1536]{1,0:T(8,128)}) %all-reduce.7.cloned.1.call-update) | async-done | bytes 313360 | tf_op jit(solution)/shard_map/psum | solution.py:91
  652.0 1.7 multiply_reduce_fusion.54
  653.7 5.5 psum.70
  660.0 1.7 broadcast_multiply_fusion.1
  661.7 5.5 fusion.2
  667.2 20.6 %all-reduce.9.cloned.1.call-done = f32[51,1536]{1,0:T(8,128)} async-done(((f32[51,1536]{1,0:T(8,128)}), f32[51,1536]{1,0:T(8,128)}) %all-reduce.9.cloned.1.call-update) | async-done | bytes 313360 | tf_op jit(solution)/shard_map/psum | solution.py:94
  687.9 1.0 broadcast_multiply_fusion
  688.9 0.6 slice_reduce_fusion
  689.5 0.8 reshape.170
  (89 shorter events, 1.0 us)
Async XLA Ops:
  7.2 201.4 %all-gather.3.cloned.1.call-start = ((), (), s32[]{:S(2)}) async-start(), calls=%async_computation.3 | async-start | bytes 24772608 | tf_op jit(solution)/shard_map/all_gather | solution.py:53
  11.6 0.7 copy-start.9
  11.6 1.0 copy-start.2
  11.6 2.6 copy-start
  11.7 306.2 %reduce-scatter.2.cloned.1.call-start = ((), (), s32[]{:S(2)}) async-start(), calls=%async_computation.4 | async-start | bytes 12386304 | tf_op jit(solution)/shard_map/reduce_scatter | solution.py:55
  47.9 0.6 copy-start.3
  47.9 0.6 copy-start.5
  325.5 5.0 copy-start.10
  325.5 58.1 %all-to-all-start = ((bf16[8,36,3584]{2,1,0:T(8,128)(2,1)}), bf16[8,36,3584]{2,1,0:T(8,128)(2,1)}, u32[]{:S(2)}, u32[]{:S(2)}) async-start(bf16[8,36,3584]{2,1,0:T(8,128)(2,1)} %all_to_all.14), calls=%async_computation.1 | async-start | bytes 4587520 | tf_op jit(solution)/shard_map/all_to_all | solution.py:58
  330.3 213.5 %all-gather.5.cloned.1.call-start = ((), (), s32[]{:S(2)}) async-start(), calls=%async_computation.5 | async-start | bytes 6193152 | tf_op jit(solution)/shard_map/all_gather | solution.py:71
  387.7 9.2 %copy-start.7 = (f32[3584]{0:T(1024)S(1)}, f32[3584]{0:T(1024)}, u32[]{:S(2)}) copy-start(f32[3584]{0:T(1024)} %param.18) | copy-start | bytes 43012
  485.6 58.1 %copy-start.8 = (f32[1536]{0:T(1024)S(1)}, f32[1536]{0:T(1024)}, u32[]{:S(2)}) copy-start(f32[1536]{0:T(1024)} %param.13) | copy-start | bytes 18436
  489.6 162.4 %all-reduce.7.cloned.1.call-start = ((), (), s32[]{:S(2)}) async-start(), calls=%async_computation.6 | async-start | bytes 688128 | tf_op jit(solution)/shard_map/psum | solution.py:91
  557.0 2.8 copy-start.4
  557.0 2.8 copy-start.6
  580.3 6.4 copy-start.1
  597.6 90.2 %all-reduce.9.cloned.1.call-start = ((), (), s32[]{:S(2)}) async-start(), calls=%async_computation.7 | async-start | bytes 688128 | tf_op jit(solution)/shard_map/psum | solution.py:94
Sparse Core Ops, SparseCore 0:
  11.8 196.7 all-gather.2
  221.8 96.0 reduce-scatter.1
  489.8 53.9 all-gather.4
  597.7 54.2 all-reduce.6
  661.8 25.9 all-reduce.8
where the time goes:
time: 698 us; the launch traced here: 697 us
  waiting for transfers between devices  434 us (62%)
  blocking collectives  85.4 us (12%)
  other arithmetic  78 us (11%)
  local copies, waits for them, and re-layouts  53.2 us (8%)
  matrix products  26.4 us (4%)
  between operations  15 us (2%)
    all_gather x1, waiting for transfers between devices, on_device(): whole_weight = lax.all_gather(projector, 'sec', axis=1, tiled=True)  155 us
    reduce_scatter x1, waiting for transfers between devices, on_device(): lax.psum_scatter(partial_value, 'tp', scatter_dimension=1, tiled=True)  96.2 us
    all_to_all x1, blocking collectives, on_device(): lax.all_to_all(picked, 'sec', split_axis=0, concat_axis=0, tiled=True)  57.6 us
    psum x1, waiting for transfers between devices, on_device(): pod_sum = lax.psum(local_delta, 'sec')  54.4 us
    all_gather x1, waiting for transfers between devices, on_device(): full_grad = lax.all_gather(returned, 'tp', axis=1, tiled=True)  54 us
    all_to_all x1, waiting for transfers between devices, on_device(): lax.all_to_all(visual, 'sec', split_axis=0, concat_axis=0, tiled=True)  53.1 us
    reduce_sum x1, other arithmetic, on_device(): jnp.sum(conv_out, axis=-1)  23.6 us
    reduce_sum x3, other arithmetic, on_device(): kernel_rows.append(jnp.sum(window * grad_conv, axis=(0, 1, 2)))  21.3 us
  transfers between devices with their start and end apart: 6, of which 6 were waited for; matrix products, arithmetic and copies ran while one was open for 5% of the time, Pallas kernels for 0%

commit v1 on v0

--- a/solution.py
+++ b/solution.py
@@ -88,7 +88,9 @@
     local_delta = jnp.stack(kernel_rows + [gain_grad, bias_grad], axis=0)
     pods = lax.axis_size("outer")
     entries = 51 * channels
-    pod_sum = lax.psum(local_delta, "sec")
+    pod_sum = local_delta
+    for hop in (1, 2, 4):
+        pod_sum = pod_sum + lax.ppermute(pod_sum, "sec", [(dev, dev ^ hop) for dev in range(8)])
     norm_sq = lax.psum(jnp.sum(pod_sum * pod_sum), "tp")
     factor = jnp.minimum(1.0, 1.0 / jnp.sqrt(norm_sq / entries + 1e-06))
     average = lax.psum(pod_sum * factor, "outer") / pods

time: 698 us -> 667 us (0.956)
  waiting for transfers between devices: 434 us -> 404 us
    psum x1 -> x0, waiting for transfers between devices: 54.4 us -> none  [on_device(): pod_sum = lax.psum(local_delta, 'sec')]
    ppermute x0 -> x3, waiting for transfers between devices: none -> 24.9 us  [on_device(): lax.ppermute(pod_sum, 'sec', [(dev, dev ^ hop) for dev in range(8)])]
  transfers between devices with their start and end apart: 6 -> 8, of which waited for: 6 -> 8; matrix products, arithmetic and copies ran while one was open for 5% -> 5% of each run, Pallas kernels for 0% -> 0%
where the time goes in v1:
time: 667 us; the launch traced here: 666 us
  waiting for transfers between devices  404 us (61%)
  blocking collectives  85.4 us (13%)
  other arithmetic  76.1 us (11%)
  local copies, waits for them, and re-layouts  48.9 us (7%)
  matrix products  26.4 us (4%)
  between operations  15.1 us (2%)
  starting transfers between devices  9.65 us (1%)
    all_gather x1, waiting for transfers between devices, on_device(): whole_weight = lax.all_gather(projector, 'sec', axis=1, tiled=True)  155 us
    reduce_scatter x1, waiting for transfers between devices, on_device(): lax.psum_scatter(partial_value, 'tp', scatter_dimension=1, tiled=True)  96.2 us
    all_to_all x1, blocking collectives, on_device(): lax.all_to_all(picked, 'sec', split_axis=0, concat_axis=0, tiled=True)  57.6 us
    all_gather x1, waiting for transfers between devices, on_device(): full_grad = lax.all_gather(returned, 'tp', axis=1, tiled=True)  54 us
    all_to_all x1, waiting for transfers between devices, on_device(): lax.all_to_all(visual, 'sec', split_axis=0, concat_axis=0, tiled=True)  53.1 us
    ppermute x3, waiting for transfers between devices, on_device(): lax.ppermute(pod_sum, 'sec', [(dev, dev ^ hop) for dev in range(8)])  24.9 us
    reduce_sum x1, other arithmetic, on_device(): jnp.sum(conv_out, axis=-1)  23.6 us
    reduce_sum x3, other arithmetic, on_device(): kernel_rows.append(jnp.sum(window * grad_conv, axis=(0, 1, 2)))  21.3 us
  transfers between devices with their start and end apart: 8, of which 8 were waited for; matrix products, arithmetic and copies ran while one was open for 5% of the time, Pallas kernels for 0%

profile of v1, /device:TPU:0, one launch (start us, length us, event | category | flops | bytes accessed | tf_op | source)
XLA Modules:
  0.0 665.5 jit_solution(16785646092002685367)
XLA Ops:
  7.2 4.4 copy.22
  11.7 0.6 copy-done.9
  12.8 0.3 slice_reduce_fusion.50
  13.1 0.9 slice_reduce_fusion.49
  14.2 0.2 convert_multiply_fusion.5
  14.4 23.6 %fusion.8 = (f32[2,12,12]{2,1,0:T(8,128)S(1)}, f32[2,12,12]{2,1,0:T(8,128)S(1)}, f32[2,12,12,1536]{3,2,1,0:T(8,128)}) fusion(f32[1536]{0:T(1024)S(1)} %get-tuple-element.110, f32[1536]{0:T(1024)S(1)} %get-tuple-element.111, f32[1536]{0:T(1024)S(1)} %get-tuple-element.64, f32[1536]{0:T(1024)S(1)} %get-tuple-element.65, f32[1536]{0:T(1024)S(1)} %get-tuple-element.66, ...), kind=kLoop, calls=%fused_computation.189 | loop fusion | flops 44236224 | bytes 3842304 | tf_op jit(solution)/shard_map/reduce_sum | solution.py:43
  38.1 9.8 %all-reduce.3 = (f32[2,12,12]{2,1,0:T(8,128)S(1)}, f32[2,12,12]{2,1,0:T(8,128)S(1)}) all-reduce(f32[2,12,12]{2,1,0:T(8,128)S(1)} %get-tuple-element.58, f32[2,12,12]{2,1,0:T(8,128)S(1)} %get-tuple-element.57), channel_id=1, replica_groups=mesh['outer'=2,'sec'=8,'tp'=2] {'tp'}, use_global_device_ids=true, to_apply=%region_3.4 | all-reduce | flops 576 | bytes 4608 | tf_op jit(solution)/shard_map/psum | solution.py:42
  47.9 0.6 copy-done.3
  48.5 3.5 multiply_convert_fusion
  52.0 1.1 reshape.168
  53.1 155.4 %all-gather.3.cloned.1.call-done = bf16[1536,7168]{1,0:T(8,128)(2,1)} async-done(((bf16[1536,896]{1,0:T(8,128)(2,1)}), bf16[1536,7168]{1,0:T(8,128)(2,1)}) %all-gather.3.cloned.1.call-update) | async-done | bytes 22020112 | tf_op jit(solution)/shard_map/all_gather | solution.py:53
  208.5 13.1 %fusion.9 = f32[288,7168]{1,0:T(8,128)} fusion(bf16[288,1536]{1,0:T(8,128)(2,1)} %reshape.168, bf16[1536,7168]{1,0:T(8,128)(2,1)} %all-gather.3.cloned.1.call-done), kind=kOutput, calls=%fused_computation.190 | convolution fusion | flops 6341787648 | bytes 31162368 | tf_op jit(solution)/shard_map/dot_general | solution.py:54
  221.7 96.2 %reduce-scatter.2.cloned.1.call-done = f32[288,3584]{1,0:T(8,128)} async-done(((f32[288,7168]{1,0:T(8,128)}), f32[288,3584]{1,0:T(8,128)}) %reduce-scatter.2.cloned.1.call-update) | async-done | bytes 4128784 | tf_op jit(solution)/shard_map/reduce_scatter | solution.py:55
  317.8 3.7 convert_element_type.43
  321.6 4.0 all_to_all.14
  325.5 4.7 all-to-all-start
  330.5 53.1 %all-to-all-done = bf16[8,36,3584]{2,1,0:T(8,128)(2,1)} async-done(((bf16[8,36,3584]{2,1,0:T(8,128)(2,1)}), bf16[8,36,3584]{2,1,0:T(8,128)(2,1)}, u32[]{:S(2)}, u32[]{:S(2)}) %all-to-all-start) | async-done | bytes 2064416 | tf_op jit(solution)/shard_map/all_to_all | solution.py:58
  383.7 4.0 reshape.184
  387.7 9.2 %scatter_fusion = bf16[576,3584]{1,0:T(8,128)(2,1)} fusion(bf16[576,3584]{1,0:T(8,128)(2,1)} %copy.22, s32[288]{0:T(512)S(1)} %fusion.7, bf16[288,3584]{1,0:T(8,128)(2,1)} %reshape.184), kind=kCustom, calls=%fused_computation.1 | custom fusion | bytes 6194304 | tf_op jit(solution)/shard_map/scatter | solution.py:60
  396.9 5.4 fusion.6
  402.3 5.0 all-reduce.2
  407.3 6.7 %fusion.5 = bf16[576,3584]{1,0:T(8,128)(2,1)} fusion(bf16[576,3584]{1,0:T(8,128)(2,1)} %scatter_fusion, bf16[576,3584]{1,0:T(8,128)(2,1)} %param.19, f32[576]{0:T(1024)S(1)} %get-tuple-element.117, f32[576]{0:T(1024)S(1)} %get-tuple-element.126, f32[3584]{0:T(1024)S(1)} %copy-done.7, f32[576]{0:T(1024)S(1)} %get-tuple-element.127), kind=kLoop, calls=%fused_computation.59 | loop fusion | flops 18579456 | bytes 12407552 | tf_op jit(solution)/shard_map/sub | solution.py:68
  414.0 10.0 %gather_fusion = bf16[288,3584]{1,0:T(8,128)(2,1)} fusion(bf16[576,3584]{1,0:T(8,128)(2,1)} %fusion.5, s32[1024]{0:T(1024)S(1)} %pad_clamp_fusion), kind=kCustom, calls=%fused_computation | custom fusion | bytes 4129920 | tf_op jit(solution)/shard_map/gather | solution.py:69
  424.1 4.0 convert_element_type.48
  428.0 57.6 %all_to_all.21 = bf16[8,36,3584]{2,1,0:T(8,128)(2,1)} all-to-all(bf16[8,36,3584]{2,1,0:T(8,128)(2,1)} %convert_element_type.48), channel_id=1, replica_groups=mesh['outer'=2,'sec'=8,'tp'=2] {'sec'}, dimensions={0} | all-to-all | bytes 4128768 | tf_op jit(solution)/shard_map/all_to_all | solution.py:70
  485.6 4.0 all_to_all.18
  489.8 54.0 %all-gather.5.cloned.1.call-done = bf16[288,7168]{1,0:T(8,128)(2,1)} async-done(((bf16[288,3584]{1,0:T(8,128)(2,1)}), bf16[288,7168]{1,0:T(8,128)(2,1)}) %all-gather.5.cloned.1.call-update) | async-done | bytes 4128784 | tf_op jit(solution)/shard_map/all_gather | solution.py:71
  543.7 13.2 %multiply_reduce_fusion.53 = (f32[1536]{0:T(1024)S(1)}, f32[288]{0:T(512)S(1)}, f32[288,1536]{1,0:T(8,128)}) fusion(f32[288]{0:T(512)S(1)} %reshape.171, f32[1536]{0:T(1024)S(1)} %copy-done.8, bf16[288,7168]{1,0:T(8,128)(2,1)} %all-gather.5.cloned.1.call-done, bf16[1536,7168]{1,0:T(8,128)(2,1)} %all-gather.3.cloned.1.call-done), kind=kOutput, calls=%fused_computation.120 | convolution fusion | flops 6343555072 | bytes 27932928 | tf_op jit(solution)/shard_map/dot_general | solution.py:72
  557.0 2.8 reshape.169
  559.8 3.4 multiply_reduce_fusion
  563.2 7.4 %all-reduce.1 = (f32[2,12,12]{2,1,0:T(8,128)S(1)}, f32[2,12,12]{2,1,0:T(8,128)S(1)}) all-reduce(f32[2,12,12]{2,1,0:T(8,128)S(1)} %get-tuple-element.5, f32[2,12,12]{2,1,0:T(8,128)S(1)} %reduce_sum.529), channel_id=1, replica_groups=mesh['outer'=2,'sec'=8,'tp'=2] {'tp'}, use_global_device_ids=true, to_apply=%region_13.14 | all-reduce | flops 576 | bytes 4608 | tf_op jit(solution)/shard_map/psum | solution.py:75
  570.7 9.6 %multiply_reduce_fusion.1 = (f32[1536]{0:T(1024)S(1)}, f32[1536]{0:T(1024)S(1)}, f32[1536]{0:T(1024)S(1)}, f32[1536]{0:T(1024)S(1)}, f32[1536]{0:T(1024)S(1)}, /...) fusion(f32[2,12,12,1536]{3,2,1,0:T(8,128)S(1)} %convert_multipl, ...), kind=kLoop, calls=%fused_computation.63 | loop fusion | flops 19436544 | bytes 7200384 | tf_op jit(solution)/shard_map/reduce_sum | solution.py:85
  580.3 6.3 multiply_reduce_fusion.19
  586.6 5.4 multiply_reduce_fusion.38
  592.8 0.5 stack.207
  593.4 1.6 collective-permute-done
  595.1 1.8 collective-permute-start.1
  596.9 8.4 %collective-permute-done.1 = f32[51,1536]{1,0:T(8,128)S(1)} collective-permute-done((f32[51,1536]{1,0:T(8,128)S(1)}, f32[51,1536]{1,0:T(8,128)S(1)}, u32[]{:S(2)}, u32[]{:S(2)}) %collective-permute-start.1) | collective-permute-done | bytes 313376 | tf_op jit(solution)/shard_map/ppermute | solution.py:93
  605.3 2.7 collective-permute-start.2
  608.0 14.9 %collective-permute-done.2 = f32[51,1536]{1,0:T(8,128)S(1)} collective-permute-done((f32[51,1536]{1,0:T(8,128)S(1)}, f32[51,1536]{1,0:T(8,128)S(1)}, u32[]{:S(2)}, u32[]{:S(2)}) %collective-permute-start.2) | collective-permute-done | bytes 313376 | tf_op jit(solution)/shard_map/ppermute | solution.py:93
  622.9 0.7 multiply_reduce_fusion.54
  623.6 5.5 psum.62
  629.9 0.8 broadcast_multiply_fusion.1
  630.7 5.5 fusion.2
  636.2 20.4 %all-reduce.6.cloned.1.call-done = f32[51,1536]{1,0:T(8,128)} async-done(((f32[51,1536]{1,0:T(8,128)}), f32[51,1536]{1,0:T(8,128)}) %all-reduce.6.cloned.1.call-update) | async-done | bytes 313360 | tf_op jit(solution)/shard_map/psum | solution.py:96
  656.6 1.0 broadcast_multiply_fusion
  657.6 0.6 slice_reduce_fusion
  658.2 0.8 reshape.170
  (94 shorter events, 1.8 us)
Async XLA Ops:
  7.2 201.4 %all-gather.3.cloned.1.call-start = ((), (), s32[]{:S(2)}) async-start(), calls=%async_computation.3 | async-start | bytes 24772608 | tf_op jit(solution)/shard_map/all_gather | solution.py:53
  11.6 0.7 copy-start.9
  11.6 1.0 copy-start.2
  11.6 2.6 copy-start
  11.7 306.2 %reduce-scatter.2.cloned.1.call-start = ((), (), s32[]{:S(2)}) async-start(), calls=%async_computation.4 | async-start | bytes 12386304 | tf_op jit(solution)/shard_map/reduce_scatter | solution.py:55
  47.9 0.6 copy-start.3
  47.9 0.6 copy-start.5
  325.5 5.0 copy-start.10
  325.5 58.1 %all-to-all-start = ((bf16[8,36,3584]{2,1,0:T(8,128)(2,1)}), bf16[8,36,3584]{2,1,0:T(8,128)(2,1)}, u32[]{:S(2)}, u32[]{:S(2)}) async-start(bf16[8,36,3584]{2,1,0:T(8,128)(2,1)} %all_to_all.14), calls=%async_computation.1 | async-start | bytes 4587520 | tf_op jit(solution)/shard_map/all_to_all | solution.py:58
  330.3 213.5 %all-gather.5.cloned.1.call-start = ((), (), s32[]{:S(2)}) async-start(), calls=%async_computation.5 | async-start | bytes 6193152 | tf_op jit(solution)/shard_map/all_gather | solution.py:71
  387.6 9.2 %copy-start.7 = (f32[3584]{0:T(1024)S(1)}, f32[3584]{0:T(1024)}, u32[]{:S(2)}) copy-start(f32[3584]{0:T(1024)} %param.18) | copy-start | bytes 43012
  485.6 58.1 %copy-start.8 = (f32[1536]{0:T(1024)S(1)}, f32[1536]{0:T(1024)}, u32[]{:S(2)}) copy-start(f32[1536]{0:T(1024)} %param.13) | copy-start | bytes 18436
  489.6 167.0 %all-reduce.6.cloned.1.call-start = ((), (), s32[]{:S(2)}) async-start(), calls=%async_computation.6 | async-start | bytes 688128 | tf_op jit(solution)/shard_map/psum | solution.py:96
  557.0 2.8 copy-start.4
  557.0 2.8 copy-start.6
  580.3 6.4 copy-start.1
  593.3 1.7 collective-permute-start
  595.1 10.2 %collective-permute-start.1 = (f32[51,1536]{1,0:T(8,128)S(1)}, f32[51,1536]{1,0:T(8,128)S(1)}, u32[]{:S(2)}, u32[]{:S(2)}) collective-permute-start(f32[51,1536]{1,0:T(8,128)S(1)} %add.263), channel_id=1, source_target_pairs={{0,4},{2,6},{4,0},{6,2},{8,12},{10,14},{12,8},{14,10},{1,5},{3,7},... | collective-permute-start | bytes 940040 | tf_op jit(solution)/shard_map/ppermute | solution.py:93
  605.3 17.6 %collective-permute-start.2 = (f32[51,1536]{1,0:T(8,128)S(1)}, f32[51,1536]{1,0:T(8,128)S(1)}, u32[]{:S(2)}, u32[]{:S(2)}) collective-permute-start(f32[51,1536]{1,0:T(8,128)S(1)} %add.264), channel_id=1, source_target_pairs={{0,8},{2,10},{4,12},{6,14},{8,0},{10,2},{12,4},{14,6},{1,9},{3,11}... | collective-permute-start | bytes 940040 | tf_op jit(solution)/shard_map/ppermute | solution.py:93
Sparse Core Ops, SparseCore 0:
  11.8 196.7 all-gather.2
  221.8 96.0 reduce-scatter.1
  489.8 53.9 all-gather.4
  630.8 25.7 all-reduce.5
